TPU v7x, 32 devices: a whole 2x2x4 slice. The times are simulated.
32 devices in a mesh: rep: 4 (over y, x), fsdp: 8 (over z, core).
Axes of the slice: x: 2, y: 2, z: 4, core: 2. Of those that a mesh axis runs over, the one named last changes fastest.
Arguments:
- inputs: bfloat16 [4, 4096, 5120], P('rep', 'fsdp'), may hold values from -6 to 6
- target: bfloat16 [4, 4096, 1024], P('rep', 'fsdp'), may hold values from -12 to 12
- norm_gain: float32 [5120], replicated, may hold values from 0.5 to 1.5
- numerators: float32 [4, 5120, 1024], P('rep', 'fsdp'), may hold values from -0.18 to 0.18
- moment: float32 [4, 5120, 1024], P('rep', 'fsdp'), may hold values from -600 to 600
- second: float32 [4, 5120, 1024], P('rep', 'fsdp'), may hold values from 1000 to 100000
- push_weight: float32 [4], P('rep'), may hold values from 0.5 to 2
- step_index: int32 [1], replicated, may hold values from 1 to 999
Outputs:
- new_numerators: float32 [4, 5120, 1024], P('rep', 'fsdp')
- new_moment: float32 [4, 5120, 1024], P('rep', 'fsdp')
- new_second: float32 [4, 5120, 1024], P('rep', 'fsdp')
- new_weight: float32 [4], P('rep')
All inputs are finite; a program needn't handle non-finite values.
Results may differ from a plain program's by a relative error of at most 0.0003.
Values may be sent and summed in bfloat16 or wider, within the bound.
A program may use at most 128 MiB of HBM per device.

v0:
```python
from functools import partial

import jax
import jax.numpy as jnp
from jax import lax
from jax.sharding import PartitionSpec as P

eps_norm = 1e-06
beta_one = 0.9
beta_two = 0.95
learn_rate = 0.001
decay_rate = 0.1
eps_adam = 1e-08


def from_partner(block, axis, bit):
    count = lax.axis_size(axis)
    route = []
    for low in range(count):
        high = low | 1 << bit
        if high != low and high < count:
            route += [(low, high), (high, low)]
    return lax.ppermute(block, axis, route)


def swap_shard(level, shard_shares, shard_weight):
    return from_partner((shard_shares, shard_weight), "rep", level)


def local(inputs, target, norm_gain, numerators, moment, second, push_weight, step_index):
    values = inputs[0].astype(jnp.float32)
    inv_rms = lax.rsqrt(jnp.mean(values * values, axis=-1, keepdims=True) + eps_norm)
    normed = (values * inv_rms * norm_gain).astype(jnp.bfloat16)
    own_weight = push_weight[0]
    current = numerators[0] / own_weight
    weight_low = current.astype(jnp.bfloat16)
    feature_cols = normed
    projected = jnp.dot(
        feature_cols,
        lax.all_gather(weight_low, "fsdp", axis=0, tiled=True),
        preferred_element_type=jnp.float32,
    )
    key_error = (projected - target[0].astype(jnp.float32)).astype(jnp.bfloat16)
    feature_cols = normed
    gradient = lax.psum_scatter(
        lax.dot_general(
            feature_cols, key_error, (((0,), (0,)), ((), ())), preferred_element_type=jnp.float32
        ),
        "fsdp",
        scatter_dimension=0,
        tiled=True,
    )
    new_moment = beta_one * moment[0] + (1.0 - beta_one) * gradient
    new_second = beta_two * second[0] + (1.0 - beta_two) * gradient * gradient
    steps_done = step_index[0].astype(jnp.float32)
    fix_one = 1.0 - jnp.power(jnp.float32(beta_one), steps_done)
    fix_two = 1.0 - jnp.power(jnp.float32(beta_two), steps_done)
    direction = new_moment / fix_one / (jnp.sqrt(new_second / fix_two) + eps_adam)
    updated = current - learn_rate * (direction + decay_rate * current)
    shares = own_weight * updated
    bit_count = lax.axis_size("rep").bit_length() - 1
    bit_index = step_index[0] % bit_count
    branches = [partial(swap_shard, level) for level in range(bit_count)]
    other_shares, other_weight = lax.switch(bit_index, branches, shares, push_weight)
    new_numerators = (shares + other_shares) * 0.5
    new_weight = (push_weight + other_weight) * 0.5
    return (new_numerators[None], new_moment[None], new_second[None], new_weight)


def solution(mesh):
    placed = (
        P("rep", "fsdp", None),
        P("rep", "fsdp", None),
        P(),
        P("rep", "fsdp", None),
        P("rep", "fsdp", None),
        P("rep", "fsdp", None),
        P("rep"),
        P(),
    )
    return jax.shard_map(
        local,
        mesh=mesh,
        in_specs=placed,
        out_specs=(
            P("rep", "fsdp", None),
            P("rep", "fsdp", None),
            P("rep", "fsdp", None),
            P("rep"),
        ),
        check_vma=False,
    )
```

profile of v0, /device:TPU:0, one launch (start us, length us, event | category | flops | bytes accessed | tf_op | source)
XLA Modules:
  0.0 420.2 jit_solution(17260243550928494518)
XLA Ops:
  7.2 0.0 all-gather.2.cloned.1.call-start
  7.9 3.1 bitcast_convert_fusion
  11.0 0.0 all-gather.2.cloned.1.call-update
  11.0 0.0 copy-start.2
  11.0 0.0 copy-start.3
  11.0 0.0 reduce-scatter.2.cloned.1.call-start
  11.1 3.7 fusion
  14.8 98.5 %all-gather.2.cloned.1.call-done = bf16[5120,1024]{1,0:T(8,128)(2,1)} async-done(((bf16[640,1024]{1,0:T(8,128)(2,1)}), bf16[5120,1024]{1,0:T(8,128)(2,1)}) %all-gather.2.cloned.1.call-update) | async-done | bytes 10485776 | tf_op jit(solution)/shard_map/all_gather | solution.py:40
  113.3 0.0 copy-done.2
  113.3 0.0 copy-done.3
  113.3 10.7 %fusion.7 = bf16[512,1024]{1,0:T(8,128)(2,1)S(1)} fusion(bf16[5120,1024]{1,0:T(8,128)(2,1)} %all-gather.2.cloned.1.call-done, bf16[1,512,5120]{2,1,0:T(8,128)(2,1)} %param.10, f32[5120]{0:T(1024)S(1)} %copy-done.3, f32[512]{0:T(512)S(1)} %add_rsqrt_fusion, bf16[1,512,1024]{2,1,0:T(8,128)(2,1)S(1)} %copy-done.2), kind=kOutput, calls=%fused_computation.16 | convolution fusion | flops 5380767744 | bytes 17848320 | tf_op jit(solution)/shard_map/dot_general | solution.py:38
  124.0 12.6 %fusion.8 = f32[5120,1024]{1,0:T(8,128)} fusion(bf16[512,1024]{1,0:T(8,128)(2,1)S(1)} %fusion.7, bf16[1,512,5120]{2,1,0:T(8,128)(2,1)} %param.10, f32[5120]{0:T(1024)S(1)} %copy-done.3, f32[512]{0:T(512)S(1)} %add_rsqrt_fusion), kind=kOutput, calls=%fused_computation.17 | convolution fusion | flops 5379194880 | bytes 27285504 | tf_op jit(solution)/shard_map/dot_general | solution.py:46
  136.6 0.0 copy-start
  136.6 0.0 reduce-scatter.2.cloned.1.call-update
  137.5 205.4 %reduce-scatter.2.cloned.1.call-done = f32[640,1024]{1,0:T(8,128)} async-done(((f32[5120,1024]{1,0:T(8,128)}), f32[640,1024]{1,0:T(8,128)}) %reduce-scatter.2.cloned.1.call-update) | async-done | bytes 2621456 | tf_op jit(solution)/shard_map/reduce_scatter | solution.py:45
  342.9 0.0 copy-done
  342.9 5.8 %fusion.15 = (f32[1,640,1024]{2,1,0:T(8,128)}, f32[640,1024]{1,0:T(8,128)S(1)}, f32[1,640,1024]{2,1,0:T(8,128)}) fusion(f32[640,1024]{1,0:T(8,128)} %reduce-scatter.2.cloned.1.call-done, f32[1,640,1024]{2,1,0:T(8,128)} %param.15, f32[]{:T(128)S(6)} %sub.14, f32[]{:T(128)S(6)} %sub.13, f32[1,640,1024]{2,1,0:T(8,128)} %param.14, ...), kind=kLoop, calls=%fused_computation.21 | loop fusion | flops 11141120 | bytes 18350092 | tf_op jit(solution)/shard_map/broadcast_in_dim | solution.py:67
  348.7 0.0 copy-start.1
  348.7 1.5 copy-done.1
  350.2 56.6 %conditional.1 = (f32[640,1024]{1,0:T(8,128)}, f32[1]{0:T(128)}) conditional(s32[]{:T(128)} %clamp.3, (f32[640,1024]{1,0:T(8,128)S(1)}, f32[1]{0:T(128)}) %tuple.16, (f32[640,1024]{1,0:T(8,128)S(1)}, f32[1]{0:T(128)}) %tuple.16), branch_computations={%region_2.3_spmd, %region_3.4_spmd} | conditional | bytes 10485872 | solution.py:64
  350.2 1.5 collective-permute-start.2
  351.7 0.5 collective-permute-start.3
  352.2 54.5 %collective-permute-done.3 = f32[1]{0:T(128)} collective-permute-done((f32[1]{0:T(128)}, f32[1]{0:T(128)}, u32[]{:S(2)}, u32[]{:S(2)}) %collective-permute-start.3) | collective-permute-done | bytes 36 | tf_op jit(solution)/shard_map/cond/branch_1_fun/ppermute | solution.py:23
  406.8 0.0 collective-permute-done.2
  406.8 4.8 %multiply_bitcast_fusion = f32[1,640,1024]{2,1,0:T(8,128)} fusion(f32[640,1024]{1,0:T(8,128)} %copy-done.1, f32[640,1024]{1,0:T(8,128)} %get-tuple-element.18), kind=kLoop, calls=%fused_computation.14 | loop fusion | flops 1310720 | bytes 7864320 | tf_op jit(solution)/shard_map/broadcast_in_dim | solution.py:67
  (1 shorter events, 0.0 us)
Async XLA Ops:
  7.2 106.1 %all-gather.2.cloned.1.call-start = ((), (), s32[]{:S(2)}) async-start(), calls=%async_computation.1 | async-start | bytes 11796480 | tf_op jit(solution)/shard_map/all_gather | solution.py:40
  11.0 102.3 %copy-start.2 = (bf16[1,512,1024]{2,1,0:T(8,128)(2,1)S(1)}, bf16[1,512,1024]{2,1,0:T(8,128)(2,1)}, u32[]{:S(2)}) copy-start(bf16[1,512,1024]{2,1,0:T(8,128)(2,1)} %param.11) | copy-start | bytes 3145732
  11.0 102.2 %copy-start.3 = (f32[5120]{0:T(1024)S(1)}, f32[5120]{0:T(1024)}, u32[]{:S(2)}) copy-start(f32[5120]{0:T(1024)} %param.12) | copy-start | bytes 61444
  11.0 331.9 %reduce-scatter.2.cloned.1.call-start = ((), (), s32[]{:S(2)}) async-start(), calls=%async_computation.2 | async-start | bytes 23592960 | tf_op jit(solution)/shard_map/reduce_scatter | solution.py:45
  136.6 206.3 %copy-start = (f32[1,640,1024]{2,1,0:T(8,128)S(1)}, f32[1,640,1024]{2,1,0:T(8,128)}, u32[]{:S(2)}) copy-start(f32[1,640,1024]{2,1,0:T(8,128)} %param.13) | copy-start | bytes 7864324
  348.7 1.5 copy-start.1
  350.2 56.6 %collective-permute-start.2 = (f32[640,1024]{1,0:T(8,128)S(1)}, f32[640,1024]{1,0:T(8,128)}, u32[]{:S(2)}, u32[]{:S(2)}) collective-permute-start(f32[640,1024]{1,0:T(8,128)S(1)} %get-tuple-element.10), channel_id=1, source_target_pairs={{0,16},{16,0},{8,24},{24,8},{1,17},{17,1},{9,25},{25,9},{2,18},{18... | collective-permute-start | bytes 7864328 | tf_op jit(solution)/shard_map/cond/branch_1_fun/ppermute | solution.py:23
  351.7 55.1 %collective-permute-start.3 = (f32[1]{0:T(128)}, f32[1]{0:T(128)}, u32[]{:S(2)}, u32[]{:S(2)}) collective-permute-start(f32[1]{0:T(128)} %get-tuple-element.11), channel_id=1, source_target_pairs={{0,16},{16,0},{8,24},{24,8},{1,17},{17,1},{9,25},{25,9},{2,18},{18... | collective-permute-start | bytes 20 | tf_op jit(solution)/shard_map/cond/branch_1_fun/ppermute | solution.py:23
Sparse Core Ops, SparseCore 0:
  11.1 102.0 all-gather.1
  136.7 206.1 reduce-scatter.1
where the time goes:
time: 420 us
  waiting for transfers between devices  358 us (85%)
  matrix products  23.3 us (6%)
  other arithmetic  17.5 us (4%)
  between operations  17.4 us (4%)
    reduce_scatter x1, waiting for transfers between devices, local(): lax.psum_scatter(lax.dot_general(feature_cols, key_error, (((0,), (0,)),...  205 us
    all_gather x1, waiting for transfers between devices, local(): lax.all_gather(weight_low, 'fsdp', axis=0, tiled=True)  98.5 us
    ppermute x2, waiting for transfers between devices, from_partner(): return lax.ppermute(block, axis, route)  54.5 us
    dot_general x1, matrix products, local(): lax.dot_general(feature_cols, key_error, (((0,), (0,)), ((), ())), prefer...  12.6 us
    dot_general x1, matrix products, local(): jnp.dot(feature_cols, lax.all_gather(weight_low, 'fsdp', axis=0, tiled=Tr...  10.7 us
  transfers between devices with their start and end apart: 4, of which 3 were waited for; matrix products, arithmetic and copies ran while one was open for 1% of the time, Pallas kernels for 0%

commit v1 on v0

v1 whole, which is shorter than its diff:
```python
from functools import partial

import jax
import jax.numpy as jnp
from jax import lax
from jax.experimental import pallas as pl
from jax.experimental.pallas import tpu as pltpu
from jax.sharding import PartitionSpec as P

eps_norm = 1e-06
beta_one = 0.9
beta_two = 0.95
learn_rate = 0.001
decay_rate = 0.1
eps_adam = 1e-08
lanes = 128
MESH = pl.DeviceIdType.MESH


def tile_of(size, top):
    best = 16
    for rows in range(16, top + 1, 16):
        if size % rows == 0:
            best = rows
    return best


def kernel(
    chips, levels, scal, bit_ref, gain_ref, x_hbm, t_hbm, n_hbm, m_hbm, s_hbm,
    on_hbm, om_hbm, os_hbm, ow_ref,
    normed, wst, wall, tgt, err, part, recv, fin, numer, mom, sec, other, wx,
    load_sem, local_sem, out_sem, wsib_s, wsib_r, tsib, nsib_s, nsib_r,
    wsend, wrecv, gsend, grecv, fsend, frecv, xsend, xrecv, psend, precv,
):
    tokens, depth = x_hbm.shape
    rows, cols = n_hbm.shape
    half = cols // 2
    chunks = half // lanes
    chip_rows = 2 * rows
    me_r = lax.axis_index("rep")
    me_f = lax.axis_index("fsdp")
    c = me_f // 2
    k = me_f % 2
    sibling = (me_r, 2 * c + 1 - k)
    left = (me_r, jnp.maximum(me_f - 2, 0))
    right = (me_r, jnp.minimum(me_f + 2, 2 * chips - 1))
    partners = []
    for level in range(levels):
        step = 1 << level
        partners.append((me_r + step * (1 - 2 * ((me_r // step) % 2)), me_f))
    has_left = c > 0
    has_right = c < chips - 1
    own_tokens = pl.ds(pl.multiple_of(k * tokens, tokens), tokens)

    load_n = pltpu.make_async_copy(n_hbm, numer, load_sem.at[0])
    load_x = pltpu.make_async_copy(x_hbm, normed.at[own_tokens], load_sem.at[1])
    load_m = pltpu.make_async_copy(m_hbm, mom, load_sem.at[2])
    load_s = pltpu.make_async_copy(s_hbm, sec, load_sem.at[3])
    own_cols = pl.ds(pl.multiple_of(k * half, half), half)
    load_t = pltpu.make_async_copy(t_hbm.at[:, own_cols], tgt.at[own_tokens], load_sem.at[4])
    load_n.start()
    load_x.start()

    barrier = pltpu.get_barrier_semaphore()

    def greet(who):
        pl.semaphore_signal(barrier, inc=1, device_id=who, device_id_type=MESH)

    greet(sibling)
    for who in partners:
        greet(who)
    pl.when(has_left)(lambda: greet(left))
    pl.when(has_right)(lambda: greet(right))

    own_weight = scal[0]
    load_n.wait()
    small = tile_of(rows, 32)

    @pl.loop(0, rows // small)
    def _(i):
        at = pl.ds(pl.multiple_of(i * small, small), small)
        wst[at, :] = (numer[at, :] / own_weight).astype(jnp.bfloat16)

    peers = 1 + levels + jnp.minimum(c, 1) + jnp.minimum(chips - 1 - c, 1)
    pl.semaphore_wait(barrier, peers)

    def remote(src, dst, send, recv_sem, who):
        return pltpu.make_async_remote_copy(
            src_ref=src, dst_ref=dst, send_sem=send, recv_sem=recv_sem,
            device_id=who, device_id_type=MESH,
        )

    my_rows = pl.ds(pl.multiple_of(c * chip_rows + k * rows, rows), rows)

    def part_cols(which, j):
        return pl.ds(pl.multiple_of(which * half + j * lanes, lanes), lanes)

    def w_sibling(j):
        return remote(
            wst.at[:, part_cols(1 - k, j)], wall.at[j, my_rows], wsib_s.at[j], wsib_r.at[j], sibling
        )

    def w_own(j):
        return pltpu.make_async_copy(
            wst.at[:, part_cols(k, j)], wall.at[j, my_rows], local_sem.at[j]
        )

    for j in range(chunks):
        w_sibling(j).start()
        w_own(j).start()

    other_cols = pl.ds(pl.multiple_of((1 - k) * half, half), half)
    send_t = remote(t_hbm.at[:, other_cols], tgt.at[own_tokens], tsib.at[0], tsib.at[1], sibling)

    def block(b):
        return pl.ds(pl.multiple_of(b * chip_rows, chip_rows), chip_rows)

    def w_right(j, b):
        return remote(
            wall.at[j, block(b)], wall.at[j, block(b)], wsend.at[0, j, b], wrecv.at[j, b], right
        )

    def w_left(j, b):
        return remote(
            wall.at[j, block(b)], wall.at[j, block(b)], wsend.at[1, j, b], wrecv.at[j, b], left
        )

    def w_step(j, s):
        if s == 0:
            w_sibling(j).wait_recv()
            w_own(j).wait()
            pl.when(has_right)(lambda: w_right(j, c).start())
            pl.when(has_left)(lambda: w_left(j, c).start())
            return

        @pl.when(c - s >= 0)
        def _():
            b = jnp.maximum(c - s, 0)
            w_right(j, b).wait_recv()
            pl.when(has_right)(lambda: w_right(j, b).start())

        @pl.when(c + s <= chips - 1)
        def _():
            b = jnp.minimum(c + s, chips - 1)
            w_left(j, b).wait_recv()
            pl.when(has_left)(lambda: w_left(j, b).start())

    def w_finish(j):
        w_sibling(j).wait_send()
        for b in range(chips):
            pl.when(has_right & (b <= c))(lambda: w_right(j, b).wait_send())
            pl.when(has_left & (b >= c))(lambda: w_left(j, b).wait_send())

    w_step(0, 0)

    load_x.wait()
    pieces = 4
    piece = tokens // pieces
    group = tile_of(piece, 16)

    def n_piece(q):
        at = pl.ds(pl.multiple_of(k * tokens + q * piece, piece), piece)
        return remote(normed.at[at], normed.at[at], nsib_s.at[q], nsib_r.at[q], sibling)

    for q in range(pieces):

        @pl.loop(0, piece // group)
        def _(i):
            start = pl.multiple_of(k * tokens + q * piece + i * group, group)
            at = pl.ds(start, group)
            values = normed[at, :].astype(jnp.float32)
            mean = jnp.mean(values * values, axis=-1, keepdims=True)
            inv_rms = lax.rsqrt(mean + eps_norm)
            normed[at, :] = (values * inv_rms * gain_ref[...]).astype(jnp.bfloat16)

        n_piece(q).start()

    load_t.start()
    send_t.start()
    load_m.start()
    load_s.start()
    wx[0] = jnp.full(wx.shape[1:], own_weight, jnp.float32)

    def p_copy(level):
        return remote(
            wx.at[0], wx.at[1 + level], psend.at[level], precv.at[level], partners[level]
        )

    for level in range(levels):
        p_copy(level).start()

    for s in range(1, chips):
        w_step(0, s)
    for q in range(pieces):
        n_piece(q).wait()
    load_t.wait()
    send_t.wait()

    ptile = tile_of(2 * tokens, 256)
    gtile = 512 if depth % 512 == 0 else lanes

    def compute(j):
        @pl.loop(0, 2 * tokens // ptile)
        def _(i):
            at = pl.ds(pl.multiple_of(i * ptile, ptile), ptile)
            projected = jnp.dot(normed[at, :], wall[j], preferred_element_type=jnp.float32)
            wanted = tgt[at, j * lanes : (j + 1) * lanes].astype(jnp.float32)
            err[at, :] = (projected - wanted).astype(jnp.bfloat16)

        @pl.loop(0, depth // gtile)
        def _(i):
            at = pl.ds(pl.multiple_of(i * gtile, gtile), gtile)
            part[j, at, :] = lax.dot_general(
                normed[:, at], err[...], (((0,), (0,)), ((), ())),
                preferred_element_type=jnp.float32,
            )

    def g_right(j, d):
        return remote(
            part.at[j, block(d)], recv.at[j, block(d + 1)], gsend.at[j, 0, d], grecv.at[j, 0, d], right
        )

    def g_left(j, d):
        return remote(
            part.at[j, block(d)], recv.at[j, block(d)], gsend.at[j, 1, d], grecv.at[j, 1, d], left
        )

    add_rows = tile_of(chip_rows, 160)

    def add_in(j, d, b):
        @pl.loop(0, chip_rows // add_rows)
        def _(i):
            to = pl.ds(pl.multiple_of(d * chip_rows + i * add_rows, add_rows), add_rows)
            src = pl.ds(pl.multiple_of(b * chip_rows + i * add_rows, add_rows), add_rows)
            part[j, to, :] = part[j, to, :] + recv[j, src, :]

    def g_first(j):
        for d in range(chips - 1, 0, -1):
            pl.when(c == 0)(lambda: g_right(j, d).start())
        for d in range(chips - 1):
            pl.when(c == chips - 1)(lambda: g_left(j, d).start())

    def g_step(j, s):
        d = chips - 1 - s

        @pl.when((c > 0) & (c < d))
        def _():
            g_right(j, d).wait_recv()
            add_in(j, d, d + 1)
            g_right(j, d).start()

        @pl.when((c < chips - 1) & (c > s))
        def _():
            g_left(j, s).wait_recv()
            add_in(j, s, s)
            g_left(j, s).start()

    def f_copy(j):
        at = pl.ds(pl.multiple_of(c * chip_rows + (1 - k) * rows, rows), rows)
        return remote(part.at[j, at], fin.at[k, j], fsend.at[j], frecv.at[j], sibling)

    def f_arrived(j):
        at = pl.ds(pl.multiple_of(c * chip_rows + (1 - k) * rows, rows), rows)
        return remote(part.at[j, at], fin.at[1 - k, j], fsend.at[j], frecv.at[j], sibling)

    def f_own(j):
        return pltpu.make_async_copy(part.at[j, my_rows], fin.at[k, j], local_sem.at[j])

    def g_final(j):
        @pl.when(has_left)
        def _():
            g_right(j, c).wait_recv()
            add_in(j, c, c + 1)

        @pl.when(has_right)
        def _():
            g_left(j, c).wait_recv()
            add_in(j, c, c)

        f_copy(j).start()
        f_own(j).start()

    def g_finish(j):
        f_copy(j).wait_send()
        for d in range(chips):
            pl.when(has_right & (d > c))(lambda: g_right(j, d).wait_send())
            pl.when(has_left & (d < c))(lambda: g_left(j, d).wait_send())

    def at_cols(h, j):
        return pl.ds(h * half + j * lanes, lanes)

    def out_m(h, j):
        cs = at_cols(h, j)
        return pltpu.make_async_copy(mom.at[:, cs], om_hbm.at[:, cs], out_sem.at[0, h, j])

    def out_s(h, j):
        cs = at_cols(h, j)
        return pltpu.make_async_copy(sec.at[:, cs], os_hbm.at[:, cs], out_sem.at[1, h, j])

    def out_n(h, j):
        cs = at_cols(h, j)
        return pltpu.make_async_copy(fin.at[h, j], on_hbm.at[:, cs], out_sem.at[2, h, j])

    def x_copy(h, j, level):
        cs = at_cols(h, j)
        return remote(
            numer.at[:, cs], other.at[level, :, cs],
            xsend.at[level, h, j], xrecv.at[level, h, j], partners[level],
        )

    adam_rows = tile_of(rows, 80)
    fix_one = scal[1]
    fix_two = scal[2]

    def adam(j):
        f_own(j).wait()
        f_arrived(j).wait_recv()
        for h in range(2):
            cs = at_cols(h, j)

            @pl.loop(0, rows // adam_rows)
            def _(i):
                at = pl.ds(pl.multiple_of(i * adam_rows, adam_rows), adam_rows)
                gradient = fin[h, j, at, :]
                new_moment = beta_one * mom[at, cs] + (1.0 - beta_one) * gradient
                new_second = beta_two * sec[at, cs] + (1.0 - beta_two) * gradient * gradient
                mom[at, cs] = new_moment
                sec[at, cs] = new_second
                current = numer[at, cs] / own_weight
                direction = new_moment / fix_one / (jnp.sqrt(new_second / fix_two) + eps_adam)
                updated = current - learn_rate * (direction + decay_rate * current)
                numer[at, cs] = own_weight * updated

            for level in range(levels):
                x_copy(h, j, level).start()
            out_m(h, j).start()
            out_s(h, j).start()

    def mix(j):
        for h in range(2):
            cs = at_cols(h, j)
            for level in range(levels):
                x_copy(h, j, level).wait_recv()

            @pl.loop(0, rows // adam_rows)
            def _(i):
                at = pl.ds(pl.multiple_of(i * adam_rows, adam_rows), adam_rows)
                theirs = other[0, at, cs]
                for level in range(1, levels):
                    theirs = jnp.where(bit_ref[0] == level, other[level, at, cs], theirs)
                fin[h, j, at, :] = (numer[at, cs] + theirs) * 0.5

            out_n(h, j).start()

    compute(0)
    g_first(0)
    load_m.wait()
    load_s.wait()
    if chunks > 1:
        for s in range(chips):
            w_step(1, s)
    for j in range(chunks):
        if j + 1 < chunks:
            compute(j + 1)
            g_first(j + 1)
        for s in range(chips):
            if j + 2 < chunks:
                w_step(j + 2, s)
            if s < chips - 1:
                g_step(j, s)
        g_final(j)
        adam(j)
        if j > 0:
            mix(j - 1)
    for level in range(levels):
        p_copy(level).wait()
    theirs = wx[1]
    for level in range(1, levels):
        theirs = jnp.where(bit_ref[0] == level, wx[1 + level], theirs)
    ow_ref[...] = (wx[0] + theirs) * 0.5
    for j in range(chunks):
        w_finish(j)
        g_finish(j)
    mix(chunks - 1)
    for j in range(chunks):
        for h in range(2):
            for level in range(levels):
                x_copy(h, j, level).wait_send()
            out_m(h, j).wait()
            out_s(h, j).wait()
            out_n(h, j).wait()


def local(inputs, target, norm_gain, numerators, moment, second, push_weight, step_index):
    chips = lax.axis_size("fsdp") // 2
    levels = lax.axis_size("rep").bit_length() - 1
    _, tokens, depth = inputs.shape
    _, rows, cols = numerators.shape
    half = cols // 2
    chunks = half // lanes
    steps_done = step_index[0].astype(jnp.float32)
    fix_one = 1.0 - jnp.power(jnp.float32(beta_one), steps_done)
    fix_two = 1.0 - jnp.power(jnp.float32(beta_two), steps_done)
    scal = jnp.stack([push_weight[0], fix_one, fix_two])
    bit = (step_index % levels).astype(jnp.int32)
    shard = jax.ShapeDtypeStruct((rows, cols), jnp.float32)
    dma = pltpu.SemaphoreType.DMA
    smem = pl.BlockSpec(memory_space=pltpu.SMEM)
    vmem = pl.BlockSpec(memory_space=pltpu.VMEM)
    hbm = pl.BlockSpec(memory_space=pltpu.HBM)
    bf16, f32 = jnp.bfloat16, jnp.float32
    flops = 2 * 2 * 2 * tokens * depth * half
    outs = pl.pallas_call(
        partial(kernel, chips, levels),
        out_shape=(shard, shard, shard, jax.ShapeDtypeStruct((8, lanes), f32)),
        in_specs=[smem, smem, vmem, hbm, hbm, hbm, hbm, hbm],
        out_specs=(hbm, hbm, hbm, vmem),
        scratch_shapes=[
            pltpu.VMEM((2 * tokens, depth), bf16),
            pltpu.VMEM((rows, cols), bf16),
            pltpu.VMEM((chunks, depth, lanes), bf16),
            pltpu.VMEM((2 * tokens, half), bf16),
            pltpu.VMEM((2 * tokens, lanes), bf16),
            pltpu.VMEM((chunks, depth, lanes), f32),
            pltpu.VMEM((chunks, depth + 2 * rows, lanes), f32),
            pltpu.VMEM((2, chunks, rows, lanes), f32),
            pltpu.VMEM((rows, cols), f32),
            pltpu.VMEM((rows, cols), f32),
            pltpu.VMEM((rows, cols), f32),
            pltpu.VMEM((levels, rows, cols), f32),
            pltpu.VMEM((1 + levels, 8, lanes), f32),
            dma((5,)),
            dma((chunks,)),
            dma((3, 2, chunks)),
            dma((chunks,)),
            dma((chunks,)),
            dma((2,)),
            dma((4,)),
            dma((4,)),
            dma((2, chunks, chips)),
            dma((chunks, chips)),
            dma((chunks, 2, chips)),
            dma((chunks, 2, chips)),
            dma((chunks,)),
            dma((chunks,)),
            dma((levels, 2, chunks)),
            dma((levels, 2, chunks)),
            dma((levels,)),
            dma((levels,)),
        ],
        compiler_params=pltpu.CompilerParams(
            collective_id=0, has_side_effects=True, vmem_limit_bytes=62 * 1024 * 1024
        ),
        cost_estimate=pl.CostEstimate(
            flops=flops, bytes_accessed=2 * tokens * depth + 28 * rows * cols, transcendentals=0
        ),
    )(scal, bit, norm_gain[None], inputs[0], target[0], numerators[0], moment[0], second[0])
    return (outs[0][None], outs[1][None], outs[2][None], outs[3][0, :1])


def solution(mesh):
    shard = P("rep", "fsdp", None)
    return jax.shard_map(
        local,
        mesh=mesh,
        in_specs=(shard, shard, P(), shard, shard, shard, P("rep"), P()),
        out_specs=(shard, shard, shard, P("rep")),
        check_vma=False,
    )
```

time: 420 us -> 404 us (0.962)
  Pallas kernels: 0 us -> 392 us
  waiting for transfers between devices: 358 us -> 0 us
  matrix products: 23.3 us -> 0 us
  other arithmetic: 17.5 us -> 0.59 us
  between operations: 17.4 us -> 2.03 us
  local copies, waits for them, and re-layouts: 1.51 us -> 9.07 us
    pallas_call x0 -> x1, Pallas kernels: none -> 392 us  [local(): pl.pallas_call(partial(kernel, chips, levels), out_shape=(shard, shard, s...]
    reduce_scatter x1 -> x0, waiting for transfers between devices: 205 us -> none  [local(): lax.psum_scatter(lax.dot_general(feature_cols, key_error, (((0,), (0,)),...]
    all_gather x1 -> x0, waiting for transfers between devices: 98.5 us -> none  [local(): lax.all_gather(weight_low, 'fsdp', axis=0, tiled=True)]
    ppermute x2 -> x0, waiting for transfers between devices: 54.5 us -> none  [from_partner(): return lax.ppermute(block, axis, route)]
    dot_general x2 -> x0, matrix products: 23.3 us -> none  [the longest x1 12.6 us: local(): lax.dot_general(feature_cols, key_error, (((0,), (0,)), ((), ())), prefer...]
    broadcast_in_dim x2 -> x0, other arithmetic: 10.7 us -> none  [the longest x1 5.81 us: local(): new_second[None]]
    unnamed x8 -> x7, local copies, waits for them, and re-layouts: 1.51 us -> 7.89 us
  transfers between devices with their start and end apart: 4 -> 0, of which waited for: 3 -> 0; matrix products, arithmetic and copies ran while one was open for 1% -> 0% of each run, Pallas kernels for 0% -> 0%
where the time goes in v1:
time: 404 us
  Pallas kernels  392 us (97%)
  local copies, waits for them, and re-layouts  9.07 us (2%)
    pallas_call x1, Pallas kernels, local(): pl.pallas_call(partial(kernel, chips, levels), out_shape=(shard, shard, s...  392 us

profile of v1, /device:TPU:0, one launch (start us, length us, event | category | flops | bytes accessed | tf_op | source)
XLA Modules:
  0.0 403.7 jit_solution(10547803102098207687)
XLA Ops:
  2.0 0.6 pad_maximum_fusion.scal
  2.6 392.0 %shard_map.111 = (f32[640,1024]{1,0:T(8,128)}, f32[640,1024]{1,0:T(8,128)}, f32[640,1024]{1,0:T(8,128)}, f32[8,128]{1,0:T(8,128)}) custom-call(f32[3]{0:T(128)} %pad_maximum_fusion.scal, s32[1]{0:T(128)S(6)} %select_n.7.bit_ref, f32[1,5120]{1,0:T(1,128)} %bitcast.18, bf16[512,5120]{1,0:T(8,128)(2,1)} %bitcast.13, bf16[512,1024]{1,0:T(8,128)(2,1)} %bitcast.17, ...), custom_call_target="tpu_custom_call" | custom-call | flops 10737418240 | bytes 23592960 | tf_op jit(solution)/shard_map/pallas_call | solution.py:413
  394.6 1.2 slice.3
  395.8 0.0 copy-start.1
  395.8 3.7 copy.17
  399.5 0.0 copy-done.1
  399.5 0.0 copy-start
  399.5 1.5 copy.18
  401.0 1.2 copy-done
  402.2 1.5 copy.19
Async XLA Ops:
  395.8 3.7 copy-start.1
  399.5 2.7 copy-start

commit v2 on v0

v2 whole, which is shorter than its diff:
```python
from functools import partial

import jax
import jax.numpy as jnp
from jax import lax
from jax.sharding import PartitionSpec as P

eps_norm = 1e-06
beta_one = 0.9
beta_two = 0.95
learn_rate = 0.001
decay_rate = 0.1
eps_adam = 1e-08
pieces = 4


def from_partner(block, axis, bit):
    count = lax.axis_size(axis)
    route = []
    for low in range(count):
        high = low | 1 << bit
        if high != low and high < count:
            route += [(low, high), (high, low)]
    return lax.ppermute(block, axis, route)


def local(inputs, target, norm_gain, numerators, moment, second, push_weight, step_index):
    values = inputs[0].astype(jnp.float32)
    inv_rms = lax.rsqrt(jnp.mean(values * values, axis=-1, keepdims=True) + eps_norm)
    normed = (values * inv_rms * norm_gain).astype(jnp.bfloat16)
    own_weight = push_weight[0]
    steps_done = step_index[0].astype(jnp.float32)
    fix_one = 1.0 - jnp.power(jnp.float32(beta_one), steps_done)
    fix_two = 1.0 - jnp.power(jnp.float32(beta_two), steps_done)
    bit_count = lax.axis_size("rep").bit_length() - 1
    bit_index = step_index[0] % bit_count
    current = numerators[0] / own_weight
    weight_low = current.astype(jnp.bfloat16)
    width = numerators.shape[2] // pieces

    def swap(block):
        theirs = from_partner(block, "rep", 0)
        for level in range(1, bit_count):
            theirs = jnp.where(bit_index == level, from_partner(block, "rep", level), theirs)
        return theirs

    whole = []
    for piece in range(pieces):
        rows = weight_low[:, piece * width : (piece + 1) * width]
        if whole:
            rows, whole[-1] = lax.optimization_barrier((rows, whole[-1]))
        whole.append(lax.all_gather(rows, "fsdp", axis=0, tiled=True))
    sums = []
    for piece in range(pieces):
        cut = slice(piece * width, (piece + 1) * width)
        projected = jnp.dot(normed, whole[piece], preferred_element_type=jnp.float32)
        key_error = (projected - target[0][:, cut].astype(jnp.float32)).astype(jnp.bfloat16)
        term = lax.dot_general(
            normed, key_error, (((0,), (0,)), ((), ())), preferred_element_type=jnp.float32
        )
        if sums:
            term, sums[-1] = lax.optimization_barrier((term, sums[-1]))
        sums.append(lax.psum_scatter(term, "fsdp", scatter_dimension=0, tiled=True))
    mixed, moments, seconds = [], [], []
    for piece in range(pieces):
        cut = slice(piece * width, (piece + 1) * width)
        gradient = sums[piece]
        new_moment = beta_one * moment[0][:, cut] + (1.0 - beta_one) * gradient
        new_second = beta_two * second[0][:, cut] + (1.0 - beta_two) * gradient * gradient
        direction = new_moment / fix_one / (jnp.sqrt(new_second / fix_two) + eps_adam)
        here = current[:, cut]
        updated = here - learn_rate * (direction + decay_rate * here)
        shares = own_weight * updated
        mixed.append((shares + swap(shares)) * 0.5)
        moments.append(new_moment)
        seconds.append(new_second)
    new_weight = (push_weight + swap(push_weight)) * 0.5
    join = partial(jnp.concatenate, axis=1)
    return (join(mixed)[None], join(moments)[None], join(seconds)[None], new_weight)


def solution(mesh):
    placed = (
        P("rep", "fsdp", None),
        P("rep", "fsdp", None),
        P(),
        P("rep", "fsdp", None),
        P("rep", "fsdp", None),
        P("rep", "fsdp", None),
        P("rep"),
        P(),
    )
    return jax.shard_map(
        local,
        mesh=mesh,
        in_specs=placed,
        out_specs=(
            P("rep", "fsdp", None),
            P("rep", "fsdp", None),
            P("rep", "fsdp", None),
            P("rep"),
        ),
        check_vma=False,
    )
```

time: 420 us -> 475 us (1.13)
  matrix products: 23.3 us -> 52 us
  waiting for transfers between devices: 358 us -> 368 us
  starting transfers between devices: 2.11 us -> 12 us
    dot_general x2 -> x4, matrix products: 23.3 us -> 52 us  [local(): lax.dot_general(normed, key_error, (((0,), (0,)), ((), ())), preferred_el...]
    all_gather x1 -> x4, waiting for transfers between devices: 98.5 us -> 123 us  [local(): whole.append(lax.all_gather(rows, 'fsdp', axis=0, tiled=True))]
    ppermute x2 -> x10, waiting for transfers between devices: 54.5 us -> 41.4 us  [from_partner(): return lax.ppermute(block, axis, route)]
    ppermute x2 -> x10, starting transfers between devices: 2.03 us -> 11.2 us  [from_partner(): return lax.ppermute(block, axis, route)]
    mul x0 -> x5, other arithmetic: none -> 8.41 us  [the longest x1 5.52 us: local(): shares = own_weight * updated]
    reduce_scatter x1 -> x4, waiting for transfers between devices: 205 us -> 204 us  [local(): sums.append(lax.psum_scatter(term, 'fsdp', scatter_dimension=0, tiled=True))]
  transfers between devices with their start and end apart: 4 -> 18, of which waited for: 3 -> 14; matrix products, arithmetic and copies ran while one was open for 1% -> 13% of each run, Pallas kernels for 0% -> 0%
where the time goes in v2:
time: 475 us; the launch traced here: 473 us
  waiting for transfers between devices  368 us (77%)
  matrix products  52 us (11%)
  other arithmetic  20.6 us (4%)
  between operations  18 us (4%)
  starting transfers between devices  12 us (3%)
    reduce_scatter x4, waiting for transfers between devices, local(): sums.append(lax.psum_scatter(term, 'fsdp', scatter_dimension=0, tiled=True))  204 us
    all_gather x4, waiting for transfers between devices, local(): whole.append(lax.all_gather(rows, 'fsdp', axis=0, tiled=True))  123 us
    dot_general x4, matrix products, local(): lax.dot_general(normed, key_error, (((0,), (0,)), ((), ())), preferred_el...  52 us
    ppermute x10, waiting for transfers between devices, from_partner(): return lax.ppermute(block, axis, route)  41.4 us
    ppermute x10, starting transfers between devices, from_partner(): return lax.ppermute(block, axis, route)  11.2 us
  transfers between devices with their start and end apart: 18, of which 14 were waited for; matrix products, arithmetic and copies ran while one was open for 13% of the time, Pallas kernels for 0%

profile of v2, /device:TPU:0, one launch (start us, length us, event | category | flops | bytes accessed | tf_op | source)
XLA Modules:
  0.0 473.0 jit_solution(2075548190188273793)
XLA Ops:
  7.9 2.4 fusion.43
  10.2 1.1 fusion.44
  11.4 36.7 %all-gather.5.cloned.1.call-done = bf16[5120,256]{1,0:T(8,128)(2,1)} async-done(((bf16[640,256]{1,0:T(8,128)(2,1)}), bf16[5120,256]{1,0:T(8,128)(2,1)}) %all-gather.5.cloned.1.call-update) | async-done | bytes 2621456 | tf_op jit(solution)/shard_map/all_gather | solution.py:52
  48.2 3.6 fusion
  51.8 13.0 %fusion.9 = f32[5120,256]{1,0:T(8,128)} fusion(bf16[5120,256]{1,0:T(8,128)(2,1)} %all-gather.5.cloned.1.call-done, bf16[512,1024]{1,0:T(8,128)(2,1)} %bitcast.39, bf16[1,512,5120]{2,1,0:T(8,128)(2,1)} %param.8, f32[5120]{0:T(1024)S(1)} %copy-done.3, f32[512]{0:T(512)S(1)} %add_rsqrt_fusion), kind=kOutput, calls=%fused_computation.23 | convolution fusion | flops 2705719296 | bytes 18657280 | tf_op jit(solution)/shard_map/dot_general | solution.py:58
  64.9 18.3 %all-gather.7.cloned.1.call-done = bf16[5120,256]{1,0:T(8,128)(2,1)} async-done(((bf16[640,256]{1,0:T(8,128)(2,1)}), bf16[5120,256]{1,0:T(8,128)(2,1)}) %all-gather.7.cloned.1.call-update) | async-done | bytes 2621456 | tf_op jit(solution)/shard_map/all_gather | solution.py:52
  83.5 13.0 %fusion.10 = f32[5120,256]{1,0:T(8,128)} fusion(bf16[5120,256]{1,0:T(8,128)(2,1)} %all-gather.7.cloned.1.call-done, bf16[512,1024]{1,0:T(8,128)(2,1)} %bitcast.40, bf16[1,512,5120]{2,1,0:T(8,128)(2,1)} %param.8, f32[5120]{0:T(1024)S(1)} %copy-done.3, f32[512]{0:T(512)S(1)} %add_rsqrt_fusion), kind=kOutput, calls=%fused_computation.24 | convolution fusion | flops 2705719296 | bytes 18657280 | tf_op jit(solution)/shard_map/dot_general | solution.py:58
  96.4 48.0 %reduce-scatter.5.cloned.1.call-done = f32[640,256]{1,0:T(8,128)} async-done(((f32[5120,256]{1,0:T(8,128)}), f32[640,256]{1,0:T(8,128)}) %reduce-scatter.5.cloned.1.call-update) | async-done | bytes 655376 | tf_op jit(solution)/shard_map/reduce_scatter | solution.py:63
  144.5 33.7 %all-gather.9.cloned.1.call-done = bf16[5120,256]{1,0:T(8,128)(2,1)} async-done(((bf16[640,256]{1,0:T(8,128)(2,1)}), bf16[5120,256]{1,0:T(8,128)(2,1)}) %all-gather.9.cloned.1.call-update) | async-done | bytes 2621456 | tf_op jit(solution)/shard_map/all_gather | solution.py:52
  178.3 13.0 %fusion.8 = f32[5120,256]{1,0:T(8,128)} fusion(bf16[5120,256]{1,0:T(8,128)(2,1)} %all-gather.9.cloned.1.call-done, bf16[512,1024]{1,0:T(8,128)(2,1)} %bitcast.41, bf16[1,512,5120]{2,1,0:T(8,128)(2,1)} %param.8, f32[5120]{0:T(1024)S(1)} %copy-done.3, f32[512]{0:T(512)S(1)} %add_rsqrt_fusion), kind=kOutput, calls=%fused_computation.22 | convolution fusion | flops 2705719296 | bytes 18657280 | tf_op jit(solution)/shard_map/dot_general | solution.py:58
  191.3 48.1 %reduce-scatter.7.cloned.1.call-done = f32[640,256]{1,0:T(8,128)} async-done(((f32[5120,256]{1,0:T(8,128)}), f32[640,256]{1,0:T(8,128)}) %reduce-scatter.7.cloned.1.call-update) | async-done | bytes 655376 | tf_op jit(solution)/shard_map/reduce_scatter | solution.py:63
  239.6 34.0 %all-gather.11.cloned.1.call-done = bf16[5120,256]{1,0:T(8,128)(2,1)} async-done(((bf16[640,256]{1,0:T(8,128)(2,1)}), bf16[5120,256]{1,0:T(8,128)(2,1)}) %all-gather.11.cloned.1.call-update) | async-done | bytes 2621456 | tf_op jit(solution)/shard_map/all_gather | solution.py:52
  273.7 13.0 %fusion.7 = f32[5120,256]{1,0:T(8,128)} fusion(bf16[5120,256]{1,0:T(8,128)(2,1)} %all-gather.11.cloned.1.call-done, bf16[512,1024]{1,0:T(8,128)(2,1)} %bitcast.42, bf16[1,512,5120]{2,1,0:T(8,128)(2,1)} %param.8, f32[5120]{0:T(1024)S(1)} %copy-done.3, f32[512]{0:T(512)S(1)} %add_rsqrt_fusion), kind=kOutput, calls=%fused_computation.21 | convolution fusion | flops 2705719296 | bytes 18657280 | tf_op jit(solution)/shard_map/dot_general | solution.py:58
  286.7 48.2 %reduce-scatter.9.cloned.1.call-done = f32[640,256]{1,0:T(8,128)} async-done(((f32[5120,256]{1,0:T(8,128)}), f32[640,256]{1,0:T(8,128)}) %reduce-scatter.9.cloned.1.call-update) | async-done | bytes 655376 | tf_op jit(solution)/shard_map/reduce_scatter | solution.py:63
  335.7 59.9 %reduce-scatter.11.cloned.1.call-done = f32[640,256]{1,0:T(8,128)} async-done(((f32[5120,256]{1,0:T(8,128)}), f32[640,256]{1,0:T(8,128)}) %reduce-scatter.11.cloned.1.call-update) | async-done | bytes 655376 | tf_op jit(solution)/shard_map/reduce_scatter | solution.py:63
  395.5 5.5 %subtract_multiply_fusion.3 = (f32[640,256]{1,0:T(8,128)}, f32[640,256]{1,0:T(8,128)S(1)}, f32[640,256]{1,0:T(8,128)}, f32[640,256]{1,0:T(8,128)}, f32[640,256]{...) fusion(f32[640,1024]{1,0:T(8,128)S(1)} %get-tuple-element.41, ...), kind=kLoop, calls=%fused_computation.48 | loop fusion | flops 10485760 | bytes 18350092 | tf_op jit(solution)/shard_map/mul | solution.py:73
  401.0 1.5 collective-permute-start
  402.6 1.5 collective-permute-start.1
  405.2 1.5 collective-permute-start.8
  406.6 23.2 %collective-permute-done.8 = f32[1]{0:T(128)} collective-permute-done((f32[1]{0:T(128)}, f32[1]{0:T(128)}, u32[]{:S(2)}, u32[]{:S(2)}) %collective-permute-start.8) | collective-permute-done | bytes 36 | tf_op jit(solution)/shard_map/ppermute | solution.py:24
  429.9 1.5 collective-permute-start.9
  431.3 2.2 collective-permute-done.9
  434.8 1.5 collective-permute-start.4
  436.3 1.5 collective-permute-start.5
  437.8 4.3 maximum_bitcast_fusion.1
  444.2 1.2 add_multiply_fusion.3
  445.5 1.4 add_multiply_fusion.2
  446.9 5.9 %collective-permute-done.4 = f32[640,256]{1,0:T(8,128)S(1)} collective-permute-done((f32[640,256]{1,0:T(8,128)}, f32[640,256]{1,0:T(8,128)S(1)}, u32[]{:S(2)}, u32[]{:S(2)}) %collective-permute-start.4) | collective-permute-done | bytes 655392 | tf_op jit(solution)/shard_map/ppermute | solution.py:24
  452.8 1.5 collective-permute-done.5
  454.4 7.5 %collective-permute-done.6 = f32[640,256]{1,0:T(8,128)S(1)} collective-permute-done((f32[640,256]{1,0:T(8,128)S(1)}, f32[640,256]{1,0:T(8,128)S(1)}, u32[]{:S(2)}, u32[]{:S(2)}) %collective-permute-start.6) | collective-permute-done | bytes 655392 | tf_op jit(solution)/shard_map/ppermute | solution.py:24
  461.8 1.2 collective-permute-done.7
  463.2 1.9 maximum_bitcast_fusion
  (35 shorter events, 4.3 us)
Async XLA Ops:
  7.2 40.9 %all-gather.5.cloned.1.call-start = ((), (), s32[]{:S(2)}) async-start(), calls=%async_computation.4 | async-start | bytes 2949120 | tf_op jit(solution)/shard_map/all_gather | solution.py:52
  10.2 41.5 %copy-start.3 = (f32[5120]{0:T(1024)S(1)}, f32[5120]{0:T(1024)}, u32[]{:S(2)}) copy-start(f32[5120]{0:T(1024)} %param.10) | copy-start | bytes 61444
  11.4 71.9 %all-gather.7.cloned.1.call-start = ((), (), s32[]{:S(2)}) async-start(), calls=%async_computation.5 | async-start | bytes 2949120 | tf_op jit(solution)/shard_map/all_gather | solution.py:52
  48.1 96.4 %reduce-scatter.5.cloned.1.call-start = ((), (), s32[]{:S(2)}) async-start(), calls=%async_computation.6 | async-start | bytes 5898240 | tf_op jit(solution)/shard_map/reduce_scatter | solution.py:63
  64.8 113.4 %all-gather.9.cloned.1.call-start = ((), (), s32[]{:S(2)}) async-start(), calls=%async_computation.7 | async-start | bytes 2949120 | tf_op jit(solution)/shard_map/all_gather | solution.py:52
  83.2 156.1 %reduce-scatter.7.cloned.1.call-start = ((), (), s32[]{:S(2)}) async-start(), calls=%async_computation.8 | async-start | bytes 5898240 | tf_op jit(solution)/shard_map/reduce_scatter | solution.py:63
  144.5 129.2 %all-gather.11.cloned.1.call-start = ((), (), s32[]{:S(2)}) async-start(), calls=%async_computation.9 | async-start | bytes 2949120 | tf_op jit(solution)/shard_map/all_gather | solution.py:52
  178.2 156.7 %reduce-scatter.9.cloned.1.call-start = ((), (), s32[]{:S(2)}) async-start(), calls=%async_computation.10 | async-start | bytes 5898240 | tf_op jit(solution)/shard_map/reduce_scatter | solution.py:63
  239.3 156.2 %reduce-scatter.11.cloned.1.call-start = ((), (), s32[]{:S(2)}) async-start(), calls=%async_computation.11 | async-start | bytes 5898240 | tf_op jit(solution)/shard_map/reduce_scatter | solution.py:63
  401.0 35.3 %collective-permute-start = (f32[640,256]{1,0:T(8,128)}, f32[640,256]{1,0:T(8,128)S(1)}, u32[]{:S(2)}, u32[]{:S(2)}) collective-permute-start(f32[640,256]{1,0:T(8,128)} %get-tuple-element.28), channel_id=1, source_target_pairs={{0,16},{16,0},{8,24},{24,8},{1,17},{17,1},{9,25},{25,9},{2,18},{18... | collective-permute-start | bytes 1966088 | tf_op jit(solution)/shard_map/ppermute | solution.py:24
  402.6 39.6 %collective-permute-start.1 = (f32[640,256]{1,0:T(8,128)}, f32[640,256]{1,0:T(8,128)}, u32[]{:S(2)}, u32[]{:S(2)}) collective-permute-start(f32[640,256]{1,0:T(8,128)} %get-tuple-element.28), channel_id=1, source_target_pairs={{0,8},{8,0},{16,24},{24,16},{1,9},{9,1},{17,25},{25,17},{2,10},{10... | collective-permute-start | bytes 1966088 | tf_op jit(solution)/shard_map/ppermute | solution.py:24
  404.1 38.7 %collective-permute-start.2 = (f32[640,256]{1,0:T(8,128)}, f32[640,256]{1,0:T(8,128)S(1)}, u32[]{:S(2)}, u32[]{:S(2)}) collective-permute-start(f32[640,256]{1,0:T(8,128)} %get-tuple-element.45), channel_id=1, source_target_pairs={{0,16},{16,0},{8,24},{24,8},{1,17},{17,1},{9,25},{25,9},{2,18},{18... | collective-permute-start | bytes 1966088 | tf_op jit(solution)/shard_map/ppermute | solution.py:24
  404.6 40.8 %collective-permute-start.3 = (f32[640,256]{1,0:T(8,128)}, f32[640,256]{1,0:T(8,128)}, u32[]{:S(2)}, u32[]{:S(2)}) collective-permute-start(f32[640,256]{1,0:T(8,128)} %get-tuple-element.45), channel_id=1, source_target_pairs={{0,8},{8,0},{16,24},{24,16},{1,9},{9,1},{17,25},{25,17},{2,10},{10... | collective-permute-start | bytes 1966088 | tf_op jit(solution)/shard_map/ppermute | solution.py:24
  405.2 24.7 %collective-permute-start.8 = (f32[1]{0:T(128)}, f32[1]{0:T(128)}, u32[]{:S(2)}, u32[]{:S(2)}) collective-permute-start(f32[1]{0:T(128)} %param.14), channel_id=1, source_target_pairs={{0,16},{16,0},{8,24},{24,8},{1,17},{17,1},{9,25},{25,9},{2,18},{18... | collective-permute-start | bytes 20 | tf_op jit(solution)/shard_map/ppermute | solution.py:24
  429.9 3.6 collective-permute-start.9
  434.8 17.9 %collective-permute-start.4 = (f32[640,256]{1,0:T(8,128)}, f32[640,256]{1,0:T(8,128)S(1)}, u32[]{:S(2)}, u32[]{:S(2)}) collective-permute-start(f32[640,256]{1,0:T(8,128)} %get-tuple-element.42), channel_id=1, source_target_pairs={{0,16},{16,0},{8,24},{24,8},{1,17},{17,1},{9,25},{25,9},{2,18},{18... | collective-permute-start | bytes 1966088 | tf_op jit(solution)/shard_map/ppermute | solution.py:24
  436.3 17.9 %collective-permute-start.5 = (f32[640,256]{1,0:T(8,128)}, f32[640,256]{1,0:T(8,128)S(1)}, u32[]{:S(2)}, u32[]{:S(2)}) collective-permute-start(f32[640,256]{1,0:T(8,128)} %get-tuple-element.42), channel_id=1, source_target_pairs={{0,8},{8,0},{16,24},{24,16},{1,9},{9,1},{17,25},{25,17},{2,10},{10... | collective-permute-start | bytes 1966088 | tf_op jit(solution)/shard_map/ppermute | solution.py:24
  437.8 4.3 copy-start
  442.2 12.1 %copy-start.1 = (f32[640,256]{1,0:T(8,128)S(1)}, f32[640,256]{1,0:T(8,128)}, u32[]{:S(2)}) copy-start(f32[640,256]{1,0:T(8,128)} %get-tuple-element.42) | copy-start | bytes 1966084
  442.2 19.6 %collective-permute-start.6 = (f32[640,256]{1,0:T(8,128)S(1)}, f32[640,256]{1,0:T(8,128)S(1)}, u32[]{:S(2)}, u32[]{:S(2)}) collective-permute-start(f32[640,256]{1,0:T(8,128)S(1)} %copy-done), channel_id=1, source_target_pairs={{0,16},{16,0},{8,24},{24,8},{1,17},{17,1},{9,25},{25,9},{2,18},{18... | collective-permute-start | bytes 1966088 | tf_op jit(solution)/shard_map/ppermute | solution.py:24
  442.8 0.9 copy-start.2
  443.7 19.4 %collective-permute-start.7 = (f32[640,256]{1,0:T(8,128)S(1)}, f32[640,256]{1,0:T(8,128)S(1)}, u32[]{:S(2)}, u32[]{:S(2)}) collective-permute-start(f32[640,256]{1,0:T(8,128)S(1)} %copy-done), channel_id=1, source_target_pairs={{0,8},{8,0},{16,24},{24,16},{1,9},{9,1},{17,25},{25,17},{2,10},{10... | collective-permute-start | bytes 1966088 | tf_op jit(solution)/shard_map/ppermute | solution.py:24
Sparse Core Ops, SparseCore 0:
  11.5 36.5 all-gather.4
  50.3 32.8 all-gather.6
  85.5 58.9 reduce-scatter.4
  146.0 32.2 all-gather.8
  180.4 58.9 reduce-scatter.6
  241.4 32.2 all-gather.10
  276.0 58.9 reduce-scatter.8
  337.2 58.2 reduce-scatter.10
